TPU v7x, 256 devices: a whole 4x4x8 slice. The times are simulated.
256 devices in a mesh: section: 16 (over x_hi, y, core), tp: 8 (over z), dp: 2 (over x_lo).
Axes of the slice: x: 4 (x_hi: 2, x_lo: 2; x = x_hi * 2 + x_lo), y: 4, z: 8, core: 2. Of those that a mesh axis runs over, the one named last changes fastest.
Arguments:
- act_first: bfloat16 [16, 128, 4096], P('section', 'dp', 'tp'), may hold values from -6 to 6
- act_fresh: bfloat16 [2, 128, 4096], P(None, 'dp', 'tp'), may hold values from -6 to 6
- grad_first: bfloat16 [16, 128, 4096], P('section', 'dp', 'tp'), may hold values from -6 to 6
- grad_fresh: bfloat16 [2, 128, 4096], P(None, 'dp', 'tp'), may hold values from -6 to 6
- stash_values: bfloat16 [16, 3, 128, 4096], P('section', None, 'dp', 'tp'), may hold values from -448 to 448
- stash_scales: bfloat16 [16, 3, 128, 32], P('section', None, 'dp', 'tp'), may hold values from 0.00049972534 to 0.0059814453
- gains: float32 [16, 4096], P('section'), may hold values from 0.1 to 1.9
- w_in: bfloat16 [16, 4096, 4096], P('section', 'dp', 'tp'), may hold values from -0.09375 to 0.09375
- w_out: bfloat16 [16, 4096, 4096], P('section', 'tp', 'dp'), may hold values from -0.09375 to 0.09375
Outputs:
- act_out: bfloat16 [16, 128, 4096], P('section', 'dp', 'tp')
- grad_out: bfloat16 [16, 128, 4096], P('section', 'dp', 'tp')
- stash_out_values: bfloat16 [16, 3, 128, 4096], P('section', None, 'dp', 'tp')
- stash_out_scales: bfloat16 [16, 3, 128, 32], P('section', None, 'dp', 'tp')
- grad_in_w: bfloat16 [16, 4096, 4096], P('section', 'dp', 'tp')
- grad_out_w: bfloat16 [16, 4096, 4096], P('section', 'tp', 'dp')
- grad_gain: float32 [16, 4096], P('section', ('tp', 'dp'))
All inputs are finite; a program needn't handle non-finite values.
Results may differ from a plain program's by a relative error of at most 0.035.
Values may be sent and summed in bfloat16 or wider, within the bound.
A program may use at most 128 MiB of HBM per device.

v0:
```python
import math

import jax
import jax.numpy as jnp
from jax import lax
from jax.sharding import PartitionSpec as P

BLOCK = 128


norm_eps = 1e-05
quant_top = 448.0
scale_eps = 1e-06
contract_rows = (((0,), (0,)), ((), ()))
contract_cols = (((1,), (1,)), ((), ()))


def partner(block, axis, stride):
    count = lax.axis_size(axis)
    route = []
    for low in range(count):
        high = low | 1 << stride
        if high != low and high < count:
            route += [(low, high), (high, low)]
    return lax.ppermute(block, axis, route)


def shifted(value, axis, by):
    size = lax.axis_size(axis)
    pairs = [(i, i + by) for i in range(size) if 0 <= i + by < size]
    return lax.ppermute(value, axis, pairs)


def quantize(inputs):
    blocks = inputs.astype(jnp.float32).reshape(
        inputs.shape[:-1] + (inputs.shape[-1] // BLOCK, BLOCK)
    )
    scales = (jnp.max(jnp.abs(blocks), axis=-1) / quant_top + scale_eps).astype(jnp.bfloat16)
    values = (blocks / scales.astype(jnp.float32)[..., None]).astype(jnp.bfloat16)
    return (values.reshape(inputs.shape), scales)


def dequantize(values, scales):
    blocks = values.astype(jnp.float32).reshape(
        values.shape[:-1] + (values.shape[-1] // BLOCK, BLOCK)
    )
    return (
        (blocks * scales.astype(jnp.float32)[..., None]).reshape(values.shape).astype(jnp.bfloat16)
    )


def feature_slice(full_rows, position, feature_width):
    return lax.dynamic_slice_in_dim(full_rows, position * feature_width, feature_width, 1)


def join_features(pieces):
    return lax.all_gather(pieces, "tp", axis=1, tiled=True)


def mirror(values, scales):
    for bit_index in range(lax.axis_size("section").bit_length() - 1):
        values, scales = partner((values, scales), "section", bit_index)
    return (values, scales)


def forward_partial(inputs, gain_full, full_in, full_out):
    widened = inputs.astype(jnp.float32)
    inv_rms = lax.rsqrt(jnp.mean(widened * widened, axis=-1, keepdims=True) + norm_eps)
    normed = (widened * inv_rms * gain_full).astype(jnp.bfloat16)
    pre_act = jnp.dot(normed, full_in, preferred_element_type=jnp.float32)
    hidden = (pre_act * jax.nn.sigmoid(pre_act)).astype(jnp.bfloat16)
    return jnp.dot(hidden, full_out, preferred_element_type=jnp.float32)


def backward_parts(restored, upstream, gain_full, full_in, full_out):
    widened = restored.astype(jnp.float32)
    inv_rms = lax.rsqrt(jnp.mean(widened * widened, axis=-1, keepdims=True) + norm_eps)
    unit_rows = widened * inv_rms
    normed = (unit_rows * gain_full).astype(jnp.bfloat16)
    pre_act = jnp.dot(normed, full_in, preferred_element_type=jnp.float32)
    gate_prob = jax.nn.sigmoid(pre_act)
    hidden = (pre_act * gate_prob).astype(jnp.bfloat16)
    grad_hidden = lax.dot_general(
        upstream, full_out, contract_cols, preferred_element_type=jnp.float32
    )
    grad_pre = (grad_hidden * gate_prob * (1.0 + pre_act * (1.0 - gate_prob))).astype(jnp.bfloat16)
    partial_value = lax.dot_general(
        grad_pre, full_in, contract_cols, preferred_element_type=jnp.float32
    )
    return (unit_rows, inv_rms, normed, hidden, grad_pre, partial_value)


def local(
    act_first, act_fresh, grad_first, grad_fresh, stash_values, stash_scales, gains, w_in, w_out
):
    section_count = lax.axis_size("section")
    section_pos = lax.axis_index("section")
    tp_pos = lax.axis_index("tp")
    tick_count = act_fresh.shape[0] + 1
    row_count = act_first.shape[1]
    feature_width = act_first.shape[2]
    grad_scale = 1.0 / math.sqrt(tick_count * row_count * lax.axis_size("dp"))
    full_in, full_out = (
        lax.all_gather(w_in[0], "dp", axis=0, tiled=True),
        lax.all_gather(w_out[0], "dp", axis=1, tiled=True),
    )
    gain_full = gains[0]
    first_act, fresh_act, first_grad, fresh_grad = (
        lax.all_gather(act_first, "tp", axis=2, tiled=True),
        lax.all_gather(act_fresh, "tp", axis=2, tiled=True),
        lax.all_gather(grad_first, "tp", axis=2, tiled=True),
        lax.all_gather(grad_fresh, "tp", axis=2, tiled=True),
    )
    parked_values, parked_scales = ([], [])
    saved_normed, saved_hidden, saved_pre, saved_upstream = ([], [], [], [])
    gain_running = jnp.zeros((feature_width,), jnp.float32)
    moved_act = first_act[0]
    moved_grad = first_grad[0]
    leaving_local = act_first[0]
    grad_input_local = grad_first[0]
    for tick_index in range(tick_count):
        if tick_index == 0:
            arriving = first_act[0]
            incoming = first_grad[0]
        else:
            arriving = jnp.where(section_pos == 0, fresh_act[tick_index - 1], moved_act)
            incoming = jnp.where(
                section_pos == section_count - 1, fresh_grad[tick_index - 1], moved_grad
            )
        act_local = feature_slice(arriving, tp_pos, feature_width)
        values, scales = quantize(act_local)
        sent_values, sent_scales = mirror(values, scales)
        parked_values.append(sent_values)
        parked_scales.append(sent_scales)
        partial_value = forward_partial(arriving, gain_full, full_in, full_out)
        summed = lax.psum(partial_value.astype(jnp.bfloat16), "tp").astype(jnp.float32)
        leaving = (arriving.astype(jnp.float32) + summed).astype(jnp.bfloat16)
        leaving_local = feature_slice(leaving, tp_pos, feature_width)
        if tick_index + 1 < tick_count:
            moved_act = shifted(leaving, "section", 1)
        stored_values, stored_scales = mirror(
            stash_values[0, tick_index], stash_scales[0, tick_index]
        )
        restored_local = dequantize(stored_values, stored_scales)
        restored = join_features(restored_local)
        unit_rows, inv_rms, normed, hidden, grad_pre, partial_value = backward_parts(
            restored, incoming, gain_full, full_in, full_out
        )
        unit_local = feature_slice(unit_rows, tp_pos, feature_width)
        grad_normed = lax.psum(partial_value.astype(jnp.bfloat16), "tp").astype(jnp.float32)
        grad_unit = grad_normed * gain_full
        center = jnp.mean(grad_unit * unit_rows, axis=-1, keepdims=True)
        grad_input = (
            incoming.astype(jnp.float32) + inv_rms * (grad_unit - unit_rows * center)
        ).astype(jnp.bfloat16)
        grad_normed_local = feature_slice(grad_normed, tp_pos, feature_width)
        grad_input_local = feature_slice(grad_input, tp_pos, feature_width)
        gain_running = gain_running + jnp.sum(grad_normed_local * unit_local, axis=0)
        saved_normed.append(normed)
        saved_hidden.append(hidden)
        saved_pre.append(grad_pre)
        saved_upstream.append(incoming)
        if tick_index + 1 < tick_count:
            moved_grad = shifted(grad_input, "section", -1)
    out_values = jnp.stack(parked_values)
    out_scales = jnp.stack(parked_scales)
    normed_all = jnp.concatenate(saved_normed, axis=0)
    pre_all = jnp.concatenate(saved_pre, axis=0)
    hidden_all = jnp.concatenate(saved_hidden, axis=0)
    upstream_all = jnp.concatenate(saved_upstream, axis=0)
    in_term = lax.dot_general(
        normed_all, pre_all, contract_rows, preferred_element_type=jnp.float32
    )
    out_term = lax.dot_general(
        upstream_all, hidden_all, contract_rows, preferred_element_type=jnp.float32
    )
    in_total, out_total, gain_total = (
        lax.psum_scatter(
            in_term.astype(jnp.bfloat16), "dp", scatter_dimension=0, tiled=True
        ).astype(jnp.float32),
        lax.psum_scatter(
            out_term.astype(jnp.bfloat16), "dp", scatter_dimension=0, tiled=True
        ).astype(jnp.float32),
        lax.psum_scatter(
            gain_running.astype(jnp.bfloat16), "dp", scatter_dimension=0, tiled=True
        ).astype(jnp.float32),
    )
    grad_in_w = (in_total * grad_scale).astype(jnp.bfloat16)
    grad_out_w = (out_total * grad_scale).astype(jnp.bfloat16).T
    return (
        leaving_local[None],
        grad_input_local[None],
        out_values[None],
        out_scales[None],
        grad_in_w[None],
        grad_out_w[None],
        (gain_total * grad_scale)[None],
    )


def solution(mesh):
    in_specs = (
        P("section", "dp", "tp"),
        P(None, "dp", "tp"),
        P("section", "dp", "tp"),
        P(None, "dp", "tp"),
        P("section", None, "dp", "tp"),
        P("section", None, "dp", "tp"),
        P("section", None),
        P("section", "dp", "tp"),
        P("section", "tp", "dp"),
    )
    out_specs = (
        P("section", "dp", "tp"),
        P("section", "dp", "tp"),
        P("section", None, "dp", "tp"),
        P("section", None, "dp", "tp"),
        P("section", "dp", "tp"),
        P("section", "tp", "dp"),
        P("section", ("tp", "dp")),
    )
    return jax.shard_map(local, mesh=mesh, in_specs=in_specs, out_specs=out_specs, check_vma=False)
```

profile of v0, /device:TPU:2, one launch (start us, length us, event | category | flops | bytes accessed | tf_op | source)
XLA Modules:
  0.0 633.8 jit_solution(2109463119524796145)
XLA Ops:
  10.0 28.9 %all_gather.28 = bf16[1,64,4096]{2,1,0:T(8,128)(2,1)S(1)} all-gather(bf16[1,64,512]{2,1,0:T(8,128)(2,1)S(1)} %copy-done.17), channel_id=1, replica_groups=mesh['section'=16,'tp'=8,'dp'=2] {'tp'}, dimensions={2}, use_global_device_ids=true | all-gather | bytes 589824 | tf_op jit(solution)/shard_map/all_gather | solution.py:109
  42.5 25.4 %all_gather.32 = bf16[1,64,4096]{2,1,0:T(8,128)(2,1)S(1)} all-gather(bf16[1,64,512]{2,1,0:T(8,128)(2,1)S(1)} %copy-done.18), channel_id=1, replica_groups=mesh['section'=16,'tp'=8,'dp'=2] {'tp'}, dimensions={2}, use_global_device_ids=true | all-gather | bytes 589824 | tf_op jit(solution)/shard_map/all_gather | solution.py:111
  67.9 2.9 collective-permute-start.26
  71.7 3.4 collective-permute-start.4
  75.3 2.2 collective-permute-start.27
  79.5 2.1 collective-permute-start.5
  84.7 2.1 collective-permute-start.23
  87.0 25.6 %all_gather.33 = bf16[64,4096]{1,0:T(8,128)(2,1)S(1)} all-gather(bf16[64,512]{1,0:T(8,128)(2,1)S(1)} %fusion.104), channel_id=1, replica_groups=mesh['section'=16,'tp'=8,'dp'=2] {'tp'}, dimensions={1}, use_global_device_ids=true | all-gather | bytes 589824 | tf_op jit(solution)/shard_map/all_gather | solution.py:57
  113.0 25.4 %all_gather.35 = bf16[64,4096]{1,0:T(8,128)(2,1)S(1)} all-gather(bf16[64,512]{1,0:T(8,128)(2,1)S(1)} %fusion.102), channel_id=1, replica_groups=mesh['section'=16,'tp'=8,'dp'=2] {'tp'}, dimensions={1}, use_global_device_ids=true | all-gather | bytes 589824 | tf_op jit(solution)/shard_map/all_gather | solution.py:57
  140.2 3.2 multiply_convert_fusion.9
  143.5 6.0 convolution_convert_fusion.7
  149.5 3.7 fusion.60
  153.2 2.2 convolution_convert_fusion.4
  157.9 3.8 collective-permute-done.12
  162.9 4.5 collective-permute-done.13
  170.5 3.0 collective-permute-done.16
  175.6 2.9 collective-permute-done.17
  178.5 2.3 collective-permute-start.18
  180.8 2.8 collective-permute-done.18
  183.8 25.6 %all_gather.34 = bf16[64,4096]{1,0:T(8,128)(2,1)S(1)} all-gather(bf16[64,512]{1,0:T(8,128)(2,1)S(1)} %fusion.103), channel_id=1, replica_groups=mesh['section'=16,'tp'=8,'dp'=2] {'tp'}, dimensions={1}, use_global_device_ids=true | all-gather | bytes 589824 | tf_op jit(solution)/shard_map/all_gather | solution.py:57
  209.6 20.7 %all-reduce.12.cloned.1.call-done = (bf16[64,4096]{1,0:T(8,128)(2,1)}, bf16[64,4096]{1,0:T(8,128)(2,1)}) async-done(((bf16[64,4096]{1,0:T(8,128)(2,1)}, bf16[64,4096]{1,0:T(8,128)(2,1)}), (bf16[64,4096]{1,0:T(8,128)(2,1)}, bf16[64,4096]{1,0:T(8,128)(2,1)})) %all-reduce.12.cloned.1.call-update) | async-done | bytes 1048592 | tf_op jit(solution)/shard_map/psum | solution.py:136
  230.4 2.1 fusion.73
  234.6 2.5 convert_multiply_fusion.6
  240.7 28.6 %all-gather.7.cloned.1.call-done = bf16[2,64,4096]{2,1,0:T(8,128)(2,1)} async-done(((bf16[2,64,512]{2,1,0:T(8,128)(2,1)}), bf16[2,64,4096]{2,1,0:T(8,128)(2,1)}) %all-gather.7.cloned.1.call-update) | async-done | bytes 1048592 | tf_op jit(solution)/shard_map/all_gather | solution.py:110
  271.2 36.9 %all-gather.9.cloned.1.call-done = bf16[2,64,4096]{2,1,0:T(8,128)(2,1)} async-done(((bf16[2,64,512]{2,1,0:T(8,128)(2,1)}), bf16[2,64,4096]{2,1,0:T(8,128)(2,1)}) %all-gather.9.cloned.1.call-update) | async-done | bytes 1048592 | tf_op jit(solution)/shard_map/all_gather | solution.py:112
  309.5 3.9 fusion.57
  313.4 2.2 convolution_convert_fusion.3
  315.6 6.0 convolution_convert_fusion.6
  321.7 74.4 %all-reduce.10.cloned.1.call-done = (bf16[64,4096]{1,0:T(8,128)(2,1)}, bf16[64,4096]{1,0:T(8,128)(2,1)}) async-done(((bf16[64,4096]{1,0:T(8,128)(2,1)}, bf16[64,4096]{1,0:T(8,128)(2,1)}), (bf16[64,4096]{1,0:T(8,128)(2,1)}, bf16[64,4096]{1,0:T(8,128)(2,1)})) %all-reduce.10.cloned.1.call-update) | async-done | bytes 1048592 | tf_op jit(solution)/shard_map/psum | solution.py:136
  405.5 2.5 collective-permute-done.19
  409.4 2.2 convolution_convert_fusion.2
  411.6 6.0 convolution_convert_fusion.5
  417.7 4.5 convolution_convert_fusion
  423.2 4.5 convolution_convert_fusion.1
  428.4 7.7 %collective-permute-start.28 = (bf16[64,512]{1,0:T(8,128)(2,1)S(1)}, bf16[64,512]{1,0:T(8,128)(2,1)S(1)}, u32[]{:S(2)}, u32[]{:S(2)}) collective-permute-start(bf16[64,512]{1,0:T(8,128)(2,1)S(1)} %fusion.101), channel_id=1, source_target_pairs={{0,16},{16,0},{32,48},{48,32},{64,80},{80,64},{96,112},{112,96},{1... | collective-permute-start | bytes 196616 | tf_op jit(solution)/shard_map/ppermute | solution.py:25
  442.6 6.1 collective-permute-start.30
  448.7 2.6 collective-permute-start.34
  457.0 2.6 collective-permute-start.42
  459.6 2.5 collective-permute-done.42
  462.1 5.1 collective-permute-done.43
  471.5 2.2 collective-permute-start.46
  481.2 2.4 collective-permute-start.31
  491.4 9.9 %all-reduce.8.cloned.1.call-done = (bf16[64,4096]{1,0:T(8,128)(2,1)}, bf16[64,4096]{1,0:T(8,128)(2,1)}) async-done(((bf16[64,4096]{1,0:T(8,128)(2,1)}, bf16[64,4096]{1,0:T(8,128)(2,1)}), (bf16[64,4096]{1,0:T(8,128)(2,1)}, bf16[64,4096]{1,0:T(8,128)(2,1)})) %all-reduce.8.cloned.1.call-update) | async-done | bytes 1048592 | tf_op jit(solution)/shard_map/psum | solution.py:136
  505.5 4.9 all-reduce
  512.6 48.0 %reduce-scatter.5.cloned.1.call-done = bf16[2048,512]{1,0:T(8,128)(2,1)} async-done(((bf16[4096,512]{1,0:T(8,128)(2,1)}), bf16[2048,512]{1,0:T(8,128)(2,1)}) %reduce-scatter.5.cloned.1.call-update) | async-done | bytes 2097168 | tf_op jit(solution)/shard_map/reduce_scatter | solution.py:181
  562.6 2.4 copy.44
  565.0 58.7 %reduce-scatter.3.cloned.1.call-done = bf16[2048,512]{1,0:T(8,128)(2,1)} async-done(((bf16[4096,512]{1,0:T(8,128)(2,1)}), bf16[2048,512]{1,0:T(8,128)(2,1)}) %reduce-scatter.3.cloned.1.call-update) | async-done | bytes 2097168 | tf_op jit(solution)/shard_map/reduce_scatter | solution.py:178
  623.7 3.3 fusion.24
  (231 shorter events, 84.9 us)
Async XLA Ops:
  7.2 133.0 %all-gather.11.cloned.1.call-start = ((), (), s32[]{:S(2)}) async-start(), calls=%async_computation.6 | async-start | bytes 6291456 | tf_op jit(solution)/shard_map/all_gather | solution.py:104
  8.0 135.5 %all-gather.13.cloned.1.call-start = ((), (), s32[]{:S(2)}) async-start(), calls=%async_computation.7 | async-start | bytes 6291456 | tf_op jit(solution)/shard_map/all_gather | solution.py:105
  8.7 221.7 %all-reduce.12.cloned.1.call-start = ((), (), s32[]{:S(2)}) async-start(), calls=%async_computation.10 | async-start | bytes 2097152 | tf_op jit(solution)/shard_map/psum | solution.py:136
  8.8 30.1 %collective-permute-start.24 = (bf16[64,4]{0,1:T(4,128)(2,1)S(1)}, bf16[64,4]{0,1:T(4,128)(2,1)S(1)}, u32[]{:S(2)}, u32[]{:S(2)}) collective-permute-start(bf16[64,4]{0,1:T(4,128)(2,1)S(1)} %get-tuple-element.59), channel_id=1, source_target_pairs={{0,16},{16,0},{32,48},{48,32},{64,80},{80,64},{96,112},{112,96},{1... | collective-permute-start | bytes 1544 | tf_op jit(solution)/shard_map/ppermute | solution.py:25
  8.9 31.6 %collective-permute-start.6 = (bf16[64,4]{0,1:T(4,128)(2,1)S(1)}, bf16[64,4]{0,1:T(4,128)(2,1)S(1)}, u32[]{:S(2)}, u32[]{:S(2)}) collective-permute-start(bf16[64,4]{0,1:T(4,128)(2,1)S(1)} %get-tuple-element.60), channel_id=1, source_target_pairs={{0,16},{16,0},{32,48},{48,32},{64,80},{80,64},{96,112},{112,96},{1... | collective-permute-start | bytes 1544 | tf_op jit(solution)/shard_map/ppermute | solution.py:25
  9.4 62.1 %collective-permute-start.20 = (bf16[64,512]{1,0:T(8,128)(2,1)S(1)}, bf16[64,512]{1,0:T(8,128)(2,1)S(1)}, u32[]{:S(2)}, u32[]{:S(2)}) collective-permute-start(bf16[64,512]{1,0:T(8,128)(2,1)S(1)} %get-tuple-element.54), channel_id=1, source_target_pairs={{0,16},{16,0},{32,48},{48,32},{64,80},{80,64},{96,112},{112,96},{1... | collective-permute-start | bytes 196616 | tf_op jit(solution)/shard_map/ppermute | solution.py:25
  9.6 31.3 %collective-permute-start.2 = (bf16[64,512]{1,0:T(8,128)(2,1)S(1)}, bf16[64,512]{1,0:T(8,128)(2,1)S(1)}, u32[]{:S(2)}, u32[]{:S(2)}) collective-permute-start(bf16[64,512]{1,0:T(8,128)(2,1)S(1)} %get-tuple-element.55), channel_id=1, source_target_pairs={{0,16},{16,0},{32,48},{48,32},{64,80},{80,64},{96,112},{112,96},{1... | collective-permute-start | bytes 196616 | tf_op jit(solution)/shard_map/ppermute | solution.py:25
  38.9 29.1 %collective-permute-start.25 = (bf16[64,4]{0,1:T(4,128)(2,1)S(1)}, bf16[64,4]{0,1:T(4,128)(2,1)S(1)}, u32[]{:S(2)}, u32[]{:S(2)}) collective-permute-start(bf16[64,4]{0,1:T(4,128)(2,1)S(1)} %collective-permute-done.24), channel_id=1, source_target_pairs={{0,32},{32,0},{16,48},{48,16},{64,96},{96,64},{80,112},{112,80},{1... | collective-permute-start | bytes 1544 | tf_op jit(solution)/shard_map/ppermute | solution.py:25
  40.5 30.4 %collective-permute-start.7 = (bf16[64,4]{0,1:T(4,128)(2,1)S(1)}, bf16[64,4]{0,1:T(4,128)(2,1)S(1)}, u32[]{:S(2)}, u32[]{:S(2)}) collective-permute-start(bf16[64,4]{0,1:T(4,128)(2,1)S(1)} %collective-permute-done.6), channel_id=1, source_target_pairs={{0,32},{32,0},{16,48},{48,16},{64,96},{96,64},{80,112},{112,80},{1... | collective-permute-start | bytes 1544 | tf_op jit(solution)/shard_map/ppermute | solution.py:25
  40.9 30.8 %collective-permute-start.3 = (bf16[64,512]{1,0:T(8,128)(2,1)S(1)}, bf16[64,512]{1,0:T(8,128)(2,1)S(1)}, u32[]{:S(2)}, u32[]{:S(2)}) collective-permute-start(bf16[64,512]{1,0:T(8,128)(2,1)S(1)} %collective-permute-done.2), channel_id=1, source_target_pairs={{0,32},{32,0},{16,48},{48,16},{64,96},{96,64},{80,112},{112,80},{1... | collective-permute-start | bytes 196616 | tf_op jit(solution)/shard_map/ppermute | solution.py:25
  67.9 7.4 %collective-permute-start.26 = (bf16[64,4]{0,1:T(4,128)(2,1)S(1)}, bf16[64,4]{0,1:T(4,128)(2,1)S(1)}, u32[]{:S(2)}, u32[]{:S(2)}) collective-permute-start(bf16[64,4]{0,1:T(4,128)(2,1)S(1)} %collective-permute-done.25), channel_id=1, source_target_pairs={{0,64},{64,0},{16,80},{80,16},{32,96},{96,32},{48,112},{112,48},{1... | collective-permute-start | bytes 1544 | tf_op jit(solution)/shard_map/ppermute | solution.py:25
  70.8 6.7 %collective-permute-start.8 = (bf16[64,4]{0,1:T(4,128)(2,1)S(1)}, bf16[64,4]{0,1:T(4,128)(2,1)S(1)}, u32[]{:S(2)}, u32[]{:S(2)}) collective-permute-start(bf16[64,4]{0,1:T(4,128)(2,1)S(1)} %collective-permute-done.7), channel_id=1, source_target_pairs={{0,64},{64,0},{16,80},{80,16},{32,96},{96,32},{48,112},{112,48},{1... | collective-permute-start | bytes 1544 | tf_op jit(solution)/shard_map/ppermute | solution.py:25
  71.5 7.5 %collective-permute-start.21 = (bf16[64,512]{1,0:T(8,128)(2,1)S(1)}, bf16[64,512]{1,0:T(8,128)(2,1)S(1)}, u32[]{:S(2)}, u32[]{:S(2)}) collective-permute-start(bf16[64,512]{1,0:T(8,128)(2,1)S(1)} %collective-permute-done.20), channel_id=1, source_target_pairs={{0,32},{32,0},{16,48},{48,16},{64,96},{96,64},{80,112},{112,80},{1... | collective-permute-start | bytes 196616 | tf_op jit(solution)/shard_map/ppermute | solution.py:25
  71.7 7.7 %collective-permute-start.4 = (bf16[64,512]{1,0:T(8,128)(2,1)S(1)}, bf16[64,512]{1,0:T(8,128)(2,1)S(1)}, u32[]{:S(2)}, u32[]{:S(2)}) collective-permute-start(bf16[64,512]{1,0:T(8,128)(2,1)S(1)} %collective-permute-done.3), channel_id=1, source_target_pairs={{0,64},{64,0},{16,80},{80,16},{32,96},{96,32},{48,112},{112,48},{1... | collective-permute-start | bytes 196616 | tf_op jit(solution)/shard_map/ppermute | solution.py:25
  75.3 7.4 %collective-permute-start.27 = (bf16[64,4]{0,1:T(4,128)(2,1)S(1)}, bf16[64,4]{0,1:T(4,128)(2,1)S(1)}, u32[]{:S(2)}, u32[]{:S(2)}) collective-permute-start(bf16[64,4]{0,1:T(4,128)(2,1)S(1)} %collective-permute-done.26), channel_id=1, source_target_pairs={{0,128},{128,0},{16,144},{144,16},{32,160},{160,32},{48,176},{176,... | collective-permute-start | bytes 1544 | tf_op jit(solution)/shard_map/ppermute | solution.py:25
  77.5 5.1 collective-permute-start.9
  79.0 5.8 collective-permute-start.22
  79.5 7.4 %collective-permute-start.5 = (bf16[64,512]{1,0:T(8,128)(2,1)S(1)}, bf16[64,512]{1,0:T(8,128)(2,1)S(1)}, u32[]{:S(2)}, u32[]{:S(2)}) collective-permute-start(bf16[64,512]{1,0:T(8,128)(2,1)S(1)} %collective-permute-done.4), channel_id=1, source_target_pairs={{0,128},{128,0},{16,144},{144,16},{32,160},{160,32},{48,176},{176,... | collective-permute-start | bytes 196616 | tf_op jit(solution)/shard_map/ppermute | solution.py:25
  84.7 28.1 %collective-permute-start.23 = (bf16[64,512]{1,0:T(8,128)(2,1)S(1)}, bf16[64,512]{1,0:T(8,128)(2,1)S(1)}, u32[]{:S(2)}, u32[]{:S(2)}) collective-permute-start(bf16[64,512]{1,0:T(8,128)(2,1)S(1)} %collective-permute-done.22), channel_id=1, source_target_pairs={{0,128},{128,0},{16,144},{144,16},{32,160},{160,32},{48,176},{176,... | collective-permute-start | bytes 196616 | tf_op jit(solution)/shard_map/ppermute | solution.py:25
  155.4 113.9 %all-gather.7.cloned.1.call-start = ((), (), s32[]{:S(2)}) async-start(), calls=%async_computation.2 | async-start | bytes 1179648 | tf_op jit(solution)/shard_map/all_gather | solution.py:110
  156.0 152.0 %all-gather.9.cloned.1.call-start = ((), (), s32[]{:S(2)}) async-start(), calls=%async_computation.3 | async-start | bytes 1179648 | tf_op jit(solution)/shard_map/all_gather | solution.py:112
  161.7 5.8 collective-permute-start.13
  167.4 16.2 %collective-permute-start.14 = (bf16[64,512]{1,0:T(8,128)(2,1)S(1)}, bf16[64,512]{1,0:T(8,128)(2,1)S(1)}, u32[]{:S(2)}, u32[]{:S(2)}) collective-permute-start(bf16[64,512]{1,0:T(8,128)(2,1)S(1)} %collective-permute-done.13), channel_id=1, source_target_pairs={{0,128},{128,0},{16,144},{144,16},{32,160},{160,32},{48,176},{176,... | collective-permute-start | bytes 196616 | tf_op jit(solution)/shard_map/ppermute | solution.py:25
  173.4 5.1 collective-permute-start.17
  175.6 220.6 %all-reduce.10.cloned.1.call-start = ((), (), s32[]{:S(2)}) async-start(), calls=%async_computation.9 | async-start | bytes 2097152 | tf_op jit(solution)/shard_map/psum | solution.py:136
  178.5 5.1 collective-permute-start.18
  232.5 36.8 %collective-permute-start = (bf16[64,4096]{1,0:T(8,128)(2,1)}, bf16[64,4096]{1,0:T(8,128)(2,1)}, u32[]{:S(2)}, u32[]{:S(2)}) collective-permute-start(bf16[64,4096]{1,0:T(8,128)(2,1)} %fusion.73), channel_id=1, source_target_pairs={{0,16},{16,32},{32,48},{48,64},{64,80},{80,96},{96,112},{112,128},... | collective-permute-start | bytes 1572872 | tf_op jit(solution)/shard_map/ppermute | solution.py:31
  238.3 69.7 %collective-permute-start.10 = (bf16[64,4096]{1,0:T(8,128)(2,1)}, bf16[64,4096]{1,0:T(8,128)(2,1)}, u32[]{:S(2)}, u32[]{:S(2)}) collective-permute-start(bf16[64,4096]{1,0:T(8,128)(2,1)} %add_convert_fusion.1), channel_id=1, source_target_pairs={{16,0},{32,16},{48,32},{64,48},{80,64},{96,80},{112,96},{128,112},... | collective-permute-start | bytes 1572872 | tf_op jit(solution)/shard_map/ppermute | solution.py:31
  321.6 179.7 %all-reduce.8.cloned.1.call-start = ((), (), s32[]{:S(2)}) async-start(), calls=%async_computation.8 | async-start | bytes 2097152 | tf_op jit(solution)/shard_map/psum | solution.py:136
  399.1 5.5 collective-permute-start.1
  402.2 5.8 collective-permute-start.19
  417.6 143.0 %reduce-scatter.5.cloned.1.call-start = ((), (), s32[]{:S(2)}) async-start(), calls=%async_computation.5 | async-start | bytes 6291456 | tf_op jit(solution)/shard_map/reduce_scatter | solution.py:181
  422.2 201.5 %reduce-scatter.3.cloned.1.call-start = ((), (), s32[]{:S(2)}) async-start(), calls=%async_computation.4 | async-start | bytes 6291456 | tf_op jit(solution)/shard_map/reduce_scatter | solution.py:178
  428.4 9.5 %collective-permute-start.28 = (bf16[64,512]{1,0:T(8,128)(2,1)S(1)}, bf16[64,512]{1,0:T(8,128)(2,1)S(1)}, u32[]{:S(2)}, u32[]{:S(2)}) collective-permute-start(bf16[64,512]{1,0:T(8,128)(2,1)S(1)} %fusion.101), channel_id=1, source_target_pairs={{0,16},{16,0},{32,48},{48,32},{64,80},{80,64},{96,112},{112,96},{1... | collective-permute-start | bytes 196616 | tf_op jit(solution)/shard_map/ppermute | solution.py:25
  439.4 9.3 %collective-permute-start.33 = (bf16[64,512]{1,0:T(8,128)(2,1)S(1)}, bf16[64,512]{1,0:T(8,128)(2,1)}, u32[]{:S(2)}, u32[]{:S(2)}) collective-permute-start(bf16[64,512]{1,0:T(8,128)(2,1)S(1)} %collective-permute-done.32), channel_id=1, source_target_pairs={{0,32},{32,0},{16,48},{48,16},{64,96},{96,64},{80,112},{112,80},{1... | collective-permute-start | bytes 196616 | tf_op jit(solution)/shard_map/ppermute | solution.py:25
  440.0 11.4 %collective-permute-start.37 = (bf16[64,512]{1,0:T(8,128)(2,1)S(1)}, bf16[64,512]{1,0:T(8,128)(2,1)}, u32[]{:S(2)}, u32[]{:S(2)}) collective-permute-start(bf16[64,512]{1,0:T(8,128)(2,1)S(1)} %collective-permute-done.36), channel_id=1, source_target_pairs={{0,32},{32,0},{16,48},{48,16},{64,96},{96,64},{80,112},{112,80},{1... | collective-permute-start | bytes 196616 | tf_op jit(solution)/shard_map/ppermute | solution.py:25
  442.6 38.5 %collective-permute-start.30 = (bf16[64,512]{1,0:T(8,128)(2,1)S(1)}, bf16[64,512]{1,0:T(8,128)(2,1)S(1)}, u32[]{:S(2)}, u32[]{:S(2)}) collective-permute-start(bf16[64,512]{1,0:T(8,128)(2,1)S(1)} %collective-permute-done.29), channel_id=1, source_target_pairs={{0,64},{64,0},{16,80},{80,16},{32,96},{96,32},{48,112},{112,48},{1... | collective-permute-start | bytes 196616 | tf_op jit(solution)/shard_map/ppermute | solution.py:25
  448.7 34.8 %collective-permute-start.34 = (bf16[64,512]{1,0:T(8,128)(2,1)}, bf16[64,512]{1,0:T(8,128)(2,1)S(1)}, u32[]{:S(2)}, u32[]{:S(2)}) collective-permute-start(bf16[64,512]{1,0:T(8,128)(2,1)} %collective-permute-done.33), channel_id=1, source_target_pairs={{0,64},{64,0},{16,80},{80,16},{32,96},{96,32},{48,112},{112,48},{1... | collective-permute-start | bytes 196616 | tf_op jit(solution)/shard_map/ppermute | solution.py:25
  451.4 33.6 %collective-permute-start.38 = (bf16[64,512]{1,0:T(8,128)(2,1)}, bf16[64,512]{1,0:T(8,128)(2,1)S(1)}, u32[]{:S(2)}, u32[]{:S(2)}) collective-permute-start(bf16[64,512]{1,0:T(8,128)(2,1)} %collective-permute-done.37), channel_id=1, source_target_pairs={{0,64},{64,0},{16,80},{80,16},{32,96},{96,32},{48,112},{112,48},{1... | collective-permute-start | bytes 196616 | tf_op jit(solution)/shard_map/ppermute | solution.py:25
  457.0 5.1 collective-permute-start.42
  462.1 5.1 collective-permute-start.43
  462.1 5.1 collective-permute-start.44
  471.5 5.2 collective-permute-start.46
  476.6 10.5 %collective-permute-start.47 = (bf16[64,4]{0,1:T(4,128)(2,1)S(1)}, bf16[64,4]{0,1:T(4,128)(2,1)S(1)}, u32[]{:S(2)}, u32[]{:S(2)}) collective-permute-start(bf16[64,4]{0,1:T(4,128)(2,1)S(1)} %collective-permute-done.46), channel_id=1, source_target_pairs={{0,128},{128,0},{16,144},{144,16},{32,160},{160,32},{48,176},{176,... | collective-permute-start | bytes 1544 | tf_op jit(solution)/shard_map/ppermute | solution.py:25
  478.7 8.4 %collective-permute-start.51 = (bf16[64,4]{0,1:T(4,128)(2,1)S(1)}, bf16[64,4]{0,1:T(4,128)(2,1)S(1)}, u32[]{:S(2)}, u32[]{:S(2)}) collective-permute-start(bf16[64,4]{0,1:T(4,128)(2,1)S(1)} %collective-permute-done.50), channel_id=1, source_target_pairs={{0,128},{128,0},{16,144},{144,16},{32,160},{160,32},{48,176},{176,... | collective-permute-start | bytes 1544 | tf_op jit(solution)/shard_map/ppermute | solution.py:25
  481.2 6.5 %collective-permute-start.31 = (bf16[64,512]{1,0:T(8,128)(2,1)S(1)}, bf16[64,512]{1,0:T(8,128)(2,1)S(1)}, u32[]{:S(2)}, u32[]{:S(2)}) collective-permute-start(bf16[64,512]{1,0:T(8,128)(2,1)S(1)} %collective-permute-done.30), channel_id=1, source_target_pairs={{0,128},{128,0},{16,144},{144,16},{32,160},{160,32},{48,176},{176,... | collective-permute-start | bytes 196616 | tf_op jit(solution)/shard_map/ppermute | solution.py:25
  483.6 5.8 collective-permute-start.35
  485.0 5.8 collective-permute-start.39
  (39 other events, 581.2 us)
Sparse Core Ops, SparseCore 0:
  9.8 64.9 all-gather.10
  76.6 62.9 all-gather.12
  155.6 74.7 all-reduce.11
  232.0 37.2 all-gather.6
  271.0 37.0 all-gather.8
  321.8 74.3 all-reduce.9
  417.8 83.5 all-reduce.7
  503.9 56.6 reduce-scatter.4
  563.3 60.3 reduce-scatter.2
where the time goes:
time: 644 us; the launch traced here: 634 us
  waiting for transfers between devices  321 us (50%)
  blocking collectives  136 us (21%)
  starting transfers between devices  75.3 us (12%)
  matrix products  47.6 us (7%)
  other arithmetic  32.4 us (5%)
  between operations  15.4 us (2%)
    psum x3, waiting for transfers between devices, local(): lax.psum(partial_value.astype(jnp.bfloat16), 'tp').astype(jnp.float32)  105 us
    all_gather x3, blocking collectives, join_features(): return lax.all_gather(pieces, 'tp', axis=1, tiled=True)  76.6 us
    ppermute x48, starting transfers between devices, partner(): return lax.ppermute(block, axis, route)  68.3 us
    reduce_scatter x1, waiting for transfers between devices, local(): lax.psum_scatter(in_term.astype(jnp.bfloat16), 'dp', scatter_dimension=0,...  58.7 us
    reduce_scatter x1, waiting for transfers between devices, local(): lax.psum_scatter(out_term.astype(jnp.bfloat16), 'dp', scatter_dimension=0...  48 us
    ppermute x48, waiting for transfers between devices, partner(): return lax.ppermute(block, axis, route)  39.6 us
    all_gather x1, waiting for transfers between devices, local(): lax.all_gather(grad_fresh, 'tp', axis=2, tiled=True)  36.9 us
    all_gather x1, blocking collectives, local(): lax.all_gather(act_first, 'tp', axis=2, tiled=True)  28.9 us
  transfers between devices with their start and end apart: 61, of which 26 were waited for; matrix products, arithmetic and copies ran while one was open for 7% of the time, Pallas kernels for 0%

commit v1 on v0

v1 whole, which is shorter than its diff:
```python
import functools
import math

import jax
import jax.numpy as jnp
from jax import lax
from jax.experimental import pallas as pl
from jax.experimental.pallas import tpu as pltpu
from jax.sharding import PartitionSpec as P

MESH = pl.DeviceIdType.MESH
BLOCK = 128
EPS = 1e-05
QUANT_TOP = 448.0
SCALE_EPS = 1e-06
F32 = jnp.float32
BF16 = jnp.bfloat16

TP = 8
DP = 2

NN = (((1,), (0,)), ((), ()))
NT = (((1,), (1,)), ((), ()))
TN = (((0,), (0,)), ((), ()))


def mm(a, b, dims):
    return lax.dot_general(a, b, dims, preferred_element_type=F32)


def sigmoid(x):
    return 1.0 / (1.0 + jnp.exp(-x))


def column_of(tile, rows):
    wide = jnp.concatenate([tile] * (rows // 8), axis=0)
    return wide.T[:, 0:1]


def tile_of(column, rows):
    return jnp.broadcast_to(column, (rows, rows)).T[0:8, :]


def kernel(
    sections, ticks, tok, width, half, inner,
    act_first, act_fresh, grad_first, grad_fresh, stash_values, stash_scales, gains, w_in_hbm, w_out_hbm,
    act_out, grad_out, out_values, out_scales, grad_in_w, grad_out_w, grad_gain,
    w_in, w_out, gain,
    A, U, R, rest, raw,
    Fp, Bp, Fr, Br, Fs, Bs, Fl, Bl,
    xs, xr, xsum_s, xsum_r,
    b_pre, b_sg, BN, BH, GP, unit_scale,
    gacc, gpieces, gsum, grecv,
    fin_a, fin_g,
    lsem, ssem, rsem,
):
    s = lax.axis_index("section")
    t = lax.axis_index("tp")
    d = lax.axis_index("dp")
    tokens = DP * tok
    rows = tokens // TP
    hw = half // 2
    model = half * DP
    fwd_width, bwd_width = half, half + 128

    quarter = lax.rem(t, 4)
    side = t // 4
    last = sections - 1

    def dev(sec, tp, dp):
        return {"section": sec, "tp": tp, "dp": dp}

    def ztp(by):
        return lax.rem(t + (by + TP), TP)

    counts = {"s": 0}
    names = {}
    pending = []

    def slot(key):
        if key not in names:
            names[key] = len(names)
        return rsem.at[names[key]]

    def push(src, dst, key, device, cond=None, is_self=None):
        sem = ssem.at[counts["s"]]
        counts["s"] += 1
        arrive = slot(key)
        copy = pltpu.make_async_remote_copy(
            src_ref=src, dst_ref=dst, send_sem=sem, recv_sem=arrive, device_id=device, device_id_type=MESH
        )
        go = cond
        if is_self is not None:
            own = is_self if cond is None else jnp.logical_and(cond, is_self)
            go = jnp.logical_not(is_self) if cond is None else jnp.logical_and(cond, jnp.logical_not(is_self))

            @pl.when(own)
            def _():
                pltpu.make_async_copy(src, dst, arrive).start()

        if go is None:
            copy.start()
        else:
            pl.when(go)(copy.start)
        pending.append((copy, go))

    def arrived(ref, key):
        pltpu.make_async_copy(ref, ref, slot(key)).wait()

    load_in = pltpu.make_async_copy(w_in_hbm.at[0], w_in, lsem.at[0])
    load_out = pltpu.make_async_copy(w_out_hbm.at[0], w_out, lsem.at[1])
    load_in.start()
    load_out.start()

    barrier = pltpu.get_barrier_semaphore()

    def greet(device, cond=None):
        def signal():
            pl.semaphore_signal(barrier, inc=1, device_id=device, device_id_type=MESH)

        if cond is None:
            signal()
        else:
            pl.when(cond)(signal)

    def is_own(i):
        return jnp.logical_and(side == d, quarter == i)

    up, down = s < last, s > 0
    for by in (1, -1, 2, -2):
        greet(dev(s, ztp(by), d))
    greet(dev(s, t, 1 - d))
    greet(dev(s + 1, t, d), up)
    greet(dev(s - 1, t, d), down)
    greet(dev(last - s, t, d))
    for i in range(4):
        greet(dev(s, 4 * d + i, side), jnp.logical_not(is_own(i)))
        greet(dev(last - s, 4 * d + i, side))
        greet(dev(last - 1 - s, 4 * d + i, side), jnp.logical_and(up, jnp.logical_not(jnp.logical_and(s == last // 2, is_own(i)))))
    self_side = (side == d).astype(jnp.int32)
    expect = (
        4 + 1 + up.astype(jnp.int32) + down.astype(jnp.int32) + 1
        + (4 - self_side) + 4
        + up.astype(jnp.int32) * (4 - self_side * (s == last // 2).astype(jnp.int32))
    )

    for k in range(ticks):
        for b in range(width // BLOCK):
            cols = pl.ds(b * BLOCK, BLOCK)
            scale = stash_scales[0, k, :, b : b + 1].astype(F32)
            rest[k, :, cols] = (stash_values[0, k, :, cols].astype(F32) * scale).astype(BF16)
    gain[...] = gains[:, pl.ds(pl.multiple_of(d * half, half), half)]

    pl.semaphore_wait(barrier, expect)

    piece_cols = pl.ds(pl.multiple_of(quarter * width, width), width)

    def to_slots(src, dst, key, sec, cond=None, other=False):
        for i in range(4):
            push(
                src.at[pl.ds(rows * i, rows)], dst.at[pl.ds(0, rows), piece_cols], key,
                dev(sec, 4 * d + i, side), cond, None if other else is_own(i),
            )

    def to_blocks(src, dst, key, sec, cond=None, own=None):
        for i in range(4):
            mine = is_own(i) if own is None else jnp.logical_and(own, is_own(i))
            push(
                src.at[pl.ds(0, rows), pl.ds(i * width, width)],
                dst.at[pl.ds(pl.multiple_of(quarter * rows, rows), rows)], key,
                dev(sec, 4 * d + i, side), cond, mine,
            )

    to_slots(act_first.at[0], A.at[0], ("A", 0), s)
    to_slots(grad_first.at[0], U.at[0], ("U", 0), s)
    for k in range(ticks):
        to_slots(rest.at[k], R.at[k], ("R", k), last - s, other=True)
    push(act_first.at[0], raw.at[0], ("raw", 0), dev(last - s, t, d))
    for k in range(1, ticks):
        to_slots(act_fresh.at[k - 1], A.at[k], ("A", k), s, s == 0)
        to_slots(grad_fresh.at[k - 1], U.at[k], ("U", k), s, s == last)

    def rows_of(j):
        return pl.ds(rows * j, rows)

    def gather_start(X, key):
        arrived(X.at[rows_of(0)], key)
        own = X.at[rows_of(0)]
        push(own, X.at[rows_of(2)], key + (2,), dev(s, ztp(-2), d))
        push(own, X.at[rows_of(6)], key + (6,), dev(s, ztp(2), d))
        push(own, X.at[rows_of(1)], key + (1,), dev(s, ztp(-1), d))
        push(own, X.at[rows_of(7)], key + (7,), dev(s, ztp(1), d))

    def gather_mid(X, key):
        arrived(X.at[rows_of(2)], key + (2,))
        push(X.at[rows_of(2)], X.at[rows_of(3)], key + (3,), dev(s, ztp(-1), d))
        push(X.at[rows_of(2), pl.ds(0, hw)], X.at[rows_of(4), pl.ds(0, hw)], key + (4,), dev(s, ztp(-2), d))
        arrived(X.at[rows_of(6)], key + (6,))
        push(X.at[rows_of(6)], X.at[rows_of(5)], key + (5,), dev(s, ztp(1), d))
        push(X.at[rows_of(6), pl.ds(hw, hw)], X.at[rows_of(4), pl.ds(hw, hw)], key + (8,), dev(s, ztp(2), d))

    def gather_end(X, key):
        for j in (1, 7, 3, 5):
            arrived(X.at[rows_of(j)], key + (j,))
        arrived(X.at[rows_of(4), pl.ds(0, hw)], key + (4,))
        arrived(X.at[rows_of(4), pl.ds(hw, hw)], key + (8,))

    def sum_start(Pk, Rk, w, key):
        push(Pk.at[rows_of(3)], Rk.at[0], key + (0,), dev(s, ztp(1), d))
        push(Pk.at[rows_of(5)], Rk.at[1], key + (1,), dev(s, ztp(-1), d))
        push(Pk.at[rows_of(4), pl.ds(0, hw)], Rk.at[2, :, pl.ds(0, hw)], key + (2,), dev(s, ztp(2), d))
        push(Pk.at[rows_of(4), pl.ds(hw, w - hw)], Rk.at[3, :, pl.ds(hw, w - hw)], key + (3,), dev(s, ztp(-2), d))
        push(Pk.at[rows_of(1)], Rk.at[4], key + (4,), dev(s, ztp(1), d))
        push(Pk.at[rows_of(7)], Rk.at[5], key + (5,), dev(s, ztp(-1), d))

    def sum_mid(Pk, Rk, Sk, w, key):
        arrived(Rk.at[0], key + (0,))
        arrived(Rk.at[2, :, pl.ds(0, hw)], key + (2,))
        lo, hi = pl.ds(0, hw), pl.ds(hw, w - hw)
        Sk[0, :, lo] = (
            Pk[rows_of(2), lo].astype(F32) + Rk[0, :, lo].astype(F32) + Rk[2, :, lo].astype(F32)
        ).astype(BF16)
        Sk[0, :, hi] = (Pk[rows_of(2), hi].astype(F32) + Rk[0, :, hi].astype(F32)).astype(BF16)
        push(Sk.at[0], Rk.at[6], key + (6,), dev(s, ztp(2), d))
        arrived(Rk.at[1], key + (1,))
        arrived(Rk.at[3, :, pl.ds(hw, w - hw)], key + (3,))
        Sk[1, :, hi] = (
            Pk[rows_of(6), hi].astype(F32) + Rk[1, :, hi].astype(F32) + Rk[3, :, hi].astype(F32)
        ).astype(BF16)
        Sk[1, :, lo] = (Pk[rows_of(6), lo].astype(F32) + Rk[1, :, lo].astype(F32)).astype(BF16)
        push(Sk.at[1], Rk.at[7], key + (7,), dev(s, ztp(-2), d))

    def sum_end(Pk, Rk, key):
        for j in (4, 5, 6, 7):
            arrived(Rk.at[j], key + (j,))
        total = Pk[rows_of(0)].astype(F32)
        for j in (4, 5, 6, 7):
            total = total + Rk[j].astype(F32)
        return total

    def swap_send(i, key):
        push(xs.at[i], xr.at[i], key, dev(s, t, 1 - d))

    def swap_sum_send(i, key):
        push(xsum_s.at[i], xsum_r.at[i], key + ("q",), dev(s, t, 1 - d))

    def project(X, i, key):
        wide = X[...].astype(F32)
        xsum_s[i] = tile_of(jnp.sum(wide * wide, axis=-1, keepdims=True), tokens)
        swap_sum_send(i, key)
        part = mm((wide * gain[...]).astype(BF16), w_in[...], NN)
        xs[i] = part.astype(BF16)
        swap_send(i, key)
        return part

    def projected(part, i, key):
        arrived(xsum_r.at[i], key + ("q",))
        arrived(xr.at[i], key)
        total = column_of(xsum_s[i] + xsum_r[i], tokens)
        inv = lax.rsqrt(total * (1.0 / model) + EPS)
        return inv * (part + xr[i].astype(F32)), inv

    def restore_project(k):
        return project(R.at[k], 3 * k + 1, ("xb", k))

    def restore_finish(k, part):
        pre, inv = projected(part, 3 * k + 1, ("xb", k))
        gate = sigmoid(pre)
        unit_scale[k] = jnp.broadcast_to(inv, (tokens, BLOCK))
        b_pre[k] = pre
        b_sg[k] = gate * (1.0 + pre * (1.0 - gate))
        BH[pl.ds(k * tokens, tokens)] = (pre * gate).astype(BF16)
        BN[pl.ds(k * tokens, tokens)] = (R[k].astype(F32) * inv * gain[...]).astype(BF16)

    def quantize(k):
        blocks = raw[k].astype(F32)
        scales = []
        for b in range(width // BLOCK):
            block = blocks[:, b * BLOCK : (b + 1) * BLOCK]
            top = jnp.max(jnp.abs(block), axis=-1, keepdims=True)
            scale = (top / QUANT_TOP + SCALE_EPS).astype(BF16)
            out_values[0, k, :, pl.ds(b * BLOCK, BLOCK)] = (block / scale.astype(F32)).astype(BF16)
            scales.append(scale.astype(F32))
        out_scales[0, k] = jnp.concatenate(scales, axis=1).astype(BF16)

    scale_out = 1.0 / math.sqrt(ticks * tokens)

    for k in range(ticks):
        gather_start(A.at[k], ("A", k))
        gather_start(U.at[k], ("U", k))
        if k == 0:
            gather_start(R.at[k], ("R", k))
            load_in.wait()
            load_out.wait()
        gather_mid(A.at[k], ("A", k))
        gather_mid(U.at[k], ("U", k))
        if k == 0:
            gather_mid(R.at[k], ("R", k))
        gather_end(A.at[k], ("A", k))
        f_part = project(A.at[k], 3 * k, ("xf", k))
        gather_end(U.at[k], ("U", k))
        g_part = mm(U[k], w_out[...], NT)
        xs[3 * k + 2] = g_part.astype(BF16)
        swap_send(3 * k + 2, ("xg", k))
        if k == 0:
            gather_end(R.at[k], ("R", k))
            r_part = restore_project(k)
        if k + 1 < ticks:
            gather_start(R.at[k + 1], ("R", k + 1))
        f_pre, _ = projected(f_part, 3 * k, ("xf", k))
        hidden = (f_pre * sigmoid(f_pre)).astype(BF16)
        Fp[k] = mm(hidden, w_out[...], NN).astype(BF16)
        sum_start(Fp.at[k], Fr.at[k], fwd_width, ("F", k))
        if k == 0:
            restore_finish(k, r_part)
        arrived(xr.at[3 * k + 2], ("xg", k))
        grad_pre = ((g_part + xr[3 * k + 2].astype(F32)) * b_sg[k]).astype(BF16)
        GP[pl.ds(k * tokens, tokens)] = grad_pre
        center = jnp.sum(grad_pre.astype(F32) * b_pre[k], axis=-1, keepdims=True)
        center_hi = center.astype(BF16).astype(F32)
        lane = lax.broadcasted_iota(jnp.int32, (tokens, BLOCK), 1)
        Bp[k, :, pl.ds(half, BLOCK)] = jnp.where(lane < BLOCK // 2, center_hi, center - center_hi).astype(BF16)
        Bp[k, :, pl.ds(0, half)] = mm(grad_pre, w_in[...], NT).astype(BF16)
        sum_start(Bp.at[k], Br.at[k], bwd_width, ("B", k))
        if k + 1 < ticks:
            gather_mid(R.at[k + 1], ("R", k + 1))
        sum_mid(Fp.at[k], Fr.at[k], Fs.at[k], fwd_width, ("F", k))
        sum_mid(Bp.at[k], Br.at[k], Bs.at[k], bwd_width, ("B", k))
        if k + 1 < ticks:
            gather_end(R.at[k + 1], ("R", k + 1))
            r_part = restore_project(k + 1)
        leaving = (A[k, rows_of(0)].astype(F32) + sum_end(Fp.at[k], Fr.at[k], ("F", k))).astype(BF16)
        Fl[k] = leaving
        if k + 1 < ticks:
            push(Fl.at[k], A.at[k + 1, rows_of(0)], ("A", k + 1), dev(s + 1, t, d), up)
            to_blocks(Fl.at[k], raw.at[k + 1], ("raw", k + 1), last - 1 - s, up, s == last // 2)
        else:
            to_blocks(Fl.at[k], fin_a, ("fin_a",), s)
        total = sum_end(Bp.at[k], Br.at[k], ("B", k))
        grad_normed = total[:, :half]
        center = total[:, half : half + 1] + total[:, half + BLOCK // 2 : half + BLOCK // 2 + 1]
        inv = unit_scale[k, rows_of(0)][:, 0:1]
        unit = R[k, rows_of(0)].astype(F32) * inv
        grads = grad_normed * gain[...] - unit * (center * (1.0 / model))
        leaving = (U[k, rows_of(0)].astype(F32) + inv * grads).astype(BF16)
        Bl[k] = leaving
        if k + 1 < ticks:
            push(Bl.at[k], U.at[k + 1, rows_of(0)], ("U", k + 1), dev(s - 1, t, d), down)
        else:
            to_blocks(Bl.at[k], fin_g, ("fin_g",), s)
        terms = grad_normed * unit
        terms = terms[0:8] + terms[8:16]
        gacc[...] = terms if k == 0 else gacc[...] + terms
        if k + 1 < ticks:
            restore_finish(k + 1, r_part)

    for i in range(4):
        push(
            gacc.at[:, pl.ds(i * width, width)], gpieces.at[quarter], ("gp",), dev(s, 4 * d + i, side), None, is_own(i)
        )
    step = 256
    for i in range(half // step):
        cols = pl.ds(i * step, step)
        grad_in_w[0, cols, :] = (mm(BN[:, cols], GP[...], TN) * scale_out).astype(BF16)
    arrived(gpieces, ("gp",))
    group = jnp.sum(gpieces[0] + gpieces[1] + gpieces[2] + gpieces[3], axis=0, keepdims=True)
    gsum[...] = jnp.broadcast_to(group.astype(BF16).astype(F32), gsum.shape)
    part_width = width // DP
    mine = pl.ds(pl.multiple_of(d * part_width, part_width), part_width)
    theirs = pl.ds(pl.multiple_of((1 - d) * part_width, part_width), part_width)
    push(gsum.at[:, theirs], grecv, ("gx",), dev(s, t, 1 - d))
    for i in range(inner // step):
        cols = pl.ds(i * step, step)
        total = mm(BH[pl.ds(0, tokens), cols], U[0], TN)
        for k in range(1, ticks):
            total = total + mm(BH[pl.ds(k * tokens, tokens), cols], U[k], TN)
        grad_out_w[0, cols, :] = (total * scale_out).astype(BF16)
    arrived(raw.at[0], ("raw", 0))
    for k in range(1, ticks):

        @pl.when(s < last)
        def _():
            arrived(raw.at[k], ("raw", k))

        @pl.when(s == last)
        def _():
            raw[k] = act_fresh[k - 1]

    for k in range(ticks):
        quantize(k)
    arrived(fin_a, ("fin_a",))
    act_out[0] = fin_a[...]
    arrived(fin_g, ("fin_g",))
    grad_out[0] = fin_g[...]
    arrived(grecv, ("gx",))
    grad_gain[...] = ((gsum[:, mine] + grecv[...]) * scale_out)[0:1]
    for copy, cond in pending:
        if cond is None:
            copy.wait_send()
        else:
            pl.when(cond)(copy.wait_send)


def local(act_first, act_fresh, grad_first, grad_fresh, stash_values, stash_scales, gains, w_in, w_out):
    sections = lax.axis_size("section")
    ticks = act_fresh.shape[0] + 1
    tok, width = act_first.shape[1:]
    half, inner = w_in.shape[1:]
    tokens = tok * DP
    rows = tokens // TP
    vmem = pl.BlockSpec(memory_space=pltpu.VMEM)
    hbm = pl.BlockSpec(memory_space=pl.ANY)
    bw = half + BLOCK
    V = pltpu.VMEM
    return pl.pallas_call(
        functools.partial(kernel, sections, ticks, tok, width, half, inner),
        out_shape=(
            jax.ShapeDtypeStruct(act_first.shape, BF16),
            jax.ShapeDtypeStruct(grad_first.shape, BF16),
            jax.ShapeDtypeStruct(stash_values.shape, BF16),
            jax.ShapeDtypeStruct(stash_scales.shape, BF16),
            jax.ShapeDtypeStruct(w_in.shape, BF16),
            jax.ShapeDtypeStruct(w_out.shape, BF16),
            jax.ShapeDtypeStruct((1, width // DP), F32),
        ),
        in_specs=[vmem] * 7 + [hbm] * 2,
        out_specs=(vmem,) * 7,
        scratch_shapes=[
            V((half, inner), BF16),
            V((inner, half), BF16),
            V((1, half), F32),
            V((ticks, tokens, half), BF16),
            V((ticks, tokens, half), BF16),
            V((ticks, tokens, half), BF16),
            V((ticks, tok, width), BF16),
            V((ticks, tok, width), BF16),
            V((ticks, tokens, half), BF16),
            V((ticks, tokens, bw), BF16),
            V((ticks, 8, rows, half), BF16),
            V((ticks, 8, rows, bw), BF16),
            V((ticks, 2, rows, half), BF16),
            V((ticks, 2, rows, bw), BF16),
            V((ticks, rows, half), BF16),
            V((ticks, rows, half), BF16),
            V((3 * ticks, tokens, inner), BF16),
            V((3 * ticks, tokens, inner), BF16),
            V((3 * ticks, 8, tokens), F32),
            V((3 * ticks, 8, tokens), F32),
            V((ticks, tokens, inner), F32),
            V((ticks, tokens, inner), F32),
            V((ticks * tokens, half), BF16),
            V((ticks * tokens, inner), BF16),
            V((ticks * tokens, inner), BF16),
            V((ticks, tokens, BLOCK), F32),
            V((8, half), F32),
            V((4, 8, width), F32),
            V((8, width), F32),
            V((8, width // DP), F32),
            V((tok, width), BF16),
            V((tok, width), BF16),
            pltpu.SemaphoreType.DMA((2,)),
            pltpu.SemaphoreType.DMA((224,)),
            pltpu.SemaphoreType.DMA((160,)),
        ],
        compiler_params=pltpu.CompilerParams(
            collective_id=1, has_side_effects=True, vmem_limit_bytes=56 * 2**20
        ),
        name="relay_window",
    )(act_first, act_fresh, grad_first, grad_fresh, stash_values, stash_scales, gains, w_in, w_out)


def solution(mesh):
    in_specs = (
        P("section", "dp", "tp"),
        P(None, "dp", "tp"),
        P("section", "dp", "tp"),
        P(None, "dp", "tp"),
        P("section", None, "dp", "tp"),
        P("section", None, "dp", "tp"),
        P("section", None),
        P("section", "dp", "tp"),
        P("section", "tp", "dp"),
    )
    out_specs = (
        P("section", "dp", "tp"),
        P("section", "dp", "tp"),
        P("section", None, "dp", "tp"),
        P("section", None, "dp", "tp"),
        P("section", "dp", "tp"),
        P("section", "tp", "dp"),
        P("section", ("tp", "dp")),
    )
    return jax.shard_map(local, mesh=mesh, in_specs=in_specs, out_specs=out_specs, check_vma=False)
```

time: 644 us -> 186 us (0.29); the launches traced: 634 us -> 185 us
  waiting for transfers between devices: 321 us -> 0 us
  Pallas kernels: 0 us -> 172 us
  blocking collectives: 136 us -> 0 us
  starting transfers between devices: 75.3 us -> 0 us
  matrix products: 47.6 us -> 0 us
  other arithmetic: 32.4 us -> 0 us
  between operations: 15.4 us -> 0.65 us
  local copies, waits for them, and re-layouts: 5.79 us -> 12.5 us
    pallas_call x0 -> x1, Pallas kernels: none -> 172 us  [local(): pl.pallas_call(functools.partial(kernel, sections, ticks, tok, width, hal...]
    all_gather x5 -> x0, blocking collectives: 131 us -> none  [the longest x3 76.6 us: join_features(): return lax.all_gather(pieces, 'tp', axis=1, tiled=True)]
    reduce_scatter x2 -> x0, waiting for transfers between devices: 107 us -> none  [the longest x1 58.7 us: local(): lax.psum_scatter(in_term.astype(jnp.bfloat16), 'dp', scatter_dimension=0,...]
    psum x3 -> x0, waiting for transfers between devices: 105 us -> none  [local(): lax.psum(partial_value.astype(jnp.bfloat16), 'tp').astype(jnp.float32)]
    ppermute x52 -> x0, starting transfers between devices: 74.9 us -> none  [the longest x48 68.3 us: partner(): return lax.ppermute(block, axis, route)]
    all_gather x4 -> x0, waiting for transfers between devices: 65.5 us -> none  [the longest x1 36.9 us: local(): lax.all_gather(grad_fresh, 'tp', axis=2, tiled=True)]
    dot_general x14 -> x0, matrix products: 47.6 us -> none  [the longest x3 18 us: forward_partial(): return jnp.dot(hidden, full_out, preferred_element_type=jnp.float32)]
    ppermute x52 -> x0, waiting for transfers between devices: 42.1 us -> none  [the longest x48 39.6 us: partner(): return lax.ppermute(block, axis, route)]
  transfers between devices with their start and end apart: 61 -> 0, of which waited for: 26 -> 0; matrix products, arithmetic and copies ran while one was open for 7% -> 0% of each run, Pallas kernels for 0% -> 0%
where the time goes in v1:
time: 186 us; the launch traced here: 185 us
  Pallas kernels  172 us (92%)
  local copies, waits for them, and re-layouts  12.5 us (7%)
    pallas_call x1, Pallas kernels, local(): pl.pallas_call(functools.partial(kernel, sections, ticks, tok, width, hal...  172 us
    unnamed x11, local copies, waits for them, and re-layouts  11.1 us

profile of v1, /device:TPU:2, one launch (start us, length us, event | category | flops | bytes accessed | tf_op | source)
XLA Modules:
  0.0 185.4 jit_solution(15236175866034030457)
XLA Ops:
  0.6 1.4 copy.16.stash_scales
  2.1 172.2 %relay_window.1 = (bf16[1,64,512]{2,1,0:T(8,128)(2,1)}, bf16[1,64,512]{2,1,0:T(8,128)(2,1)}, bf16[1,3,64,512]{3,2,1,0:T(8,128)(2,1)}, bf16[1,3,64,4]{3,2,1,0:T(8...) custom-call(bf16[1,64,512]{2,1,0:T(8,128)(2,1)} %act_first.1, ...), custom_call_target="tpu_custom_call" | custom-call | tf_op jit(solution)/shard_map/relay_window/pallas_call | solution.py:415
  174.2 1.5 copy.17
  175.7 1.5 copy.24
  177.2 1.5 copy.25
  178.7 1.6 copy.26
  180.3 0.0 copy-start
  180.3 3.2 %copy.27 = bf16[1,2048,512]{2,1,0:T(8,128)(2,1)} copy(bf16[1,2048,512]{2,1,0:T(8,128)(2,1)} %get-tuple-element.25) | data formatting | bytes 4194304
  183.5 0.0 copy-done
  183.5 0.0 copy-start.1
  183.5 1.3 copy.28
  184.8 0.0 copy-done.1
  184.8 0.6 copy.29
Async XLA Ops:
  180.3 3.2 %copy-start = (bf16[1,512,2048]{2,1,0:T(8,128)(2,1)S(1)}, bf16[1,512,2048]{2,1,0:T(8,128)(2,1)}, u32[]{:S(2)}) copy-start(bf16[1,512,2048]{2,1,0:T(8,128)(2,1)} %get-tuple-element.26) | copy-start | bytes 6291460
  183.5 1.3 copy-start.1

commit v2 on v1

--- a/solution.py
+++ b/solution.py
@@ -9,6 +9,7 @@
 from jax.sharding import PartitionSpec as P
 
 MESH = pl.DeviceIdType.MESH
+scope = jax.named_scope
 BLOCK = 128
 EPS = 1e-05
 QUANT_TOP = 448.0
@@ -43,14 +44,14 @@
 
 def kernel(
     sections, ticks, tok, width, half, inner,
-    act_first, act_fresh, grad_first, grad_fresh, stash_values, stash_scales, gains, w_in_hbm, w_out_hbm,
+    act_first_h, act_fresh_h, grad_first_h, grad_fresh_h, stash_values_h, stash_scales_h, gains_h, w_in_h, w_out_h,
     act_out, grad_out, out_values, out_scales, grad_in_w, grad_out_w, grad_gain,
-    w_in, w_out, gain,
+    act_first, act_fresh, grad_first, grad_fresh, stash_values, stash_scales, gain, w_in, w_out,
     A, U, R, rest, raw,
     Fp, Bp, Fr, Br, Fs, Bs, Fl, Bl,
     xs, xr, xsum_s, xsum_r,
     b_pre, b_sg, BN, BH, GP, unit_scale,
-    gacc, gpieces, gsum, grecv,
+    gacc, gpieces,
     fin_a, fin_g,
     lsem, ssem, rsem,
 ):
@@ -107,10 +108,23 @@
     def arrived(ref, key):
         pltpu.make_async_copy(ref, ref, slot(key)).wait()
 
-    load_in = pltpu.make_async_copy(w_in_hbm.at[0], w_in, lsem.at[0])
-    load_out = pltpu.make_async_copy(w_out_hbm.at[0], w_out, lsem.at[1])
-    load_in.start()
-    load_out.start()
+    loads = []
+    for i, (src, dst) in enumerate(
+        (
+            (stash_values_h.at[0], stash_values),
+            (stash_scales_h.at[0], stash_scales),
+            (act_first_h.at[0], act_first),
+            (grad_first_h.at[0], grad_first),
+            (gains_h.at[:, pl.ds(pl.multiple_of(d * half, half), half)], gain),
+            (act_fresh_h, act_fresh),
+            (grad_fresh_h, grad_fresh),
+            (w_in_h.at[0], w_in),
+            (w_out_h.at[0], w_out),
+        )
+    ):
+        loads.append(pltpu.make_async_copy(src, dst, lsem.at[i]))
+    for load in loads:
+        load.start()
 
     barrier = pltpu.get_barrier_semaphore()
 
@@ -130,27 +144,37 @@
     for by in (1, -1, 2, -2):
         greet(dev(s, ztp(by), d))
     greet(dev(s, t, 1 - d))
-    greet(dev(s + 1, t, d), up)
-    greet(dev(s - 1, t, d), down)
+    for by in (0, 1, -1, 2, -2):
+        greet(dev(s + 1, ztp(by), d), up)
+        greet(dev(s - 1, ztp(by), d), down)
     greet(dev(last - s, t, d))
     for i in range(4):
         greet(dev(s, 4 * d + i, side), jnp.logical_not(is_own(i)))
         greet(dev(last - s, 4 * d + i, side))
         greet(dev(last - 1 - s, 4 * d + i, side), jnp.logical_and(up, jnp.logical_not(jnp.logical_and(s == last // 2, is_own(i)))))
+    for i in range(TP):
+        greet(dev(s, i, side), jnp.logical_not(jnp.logical_and(side == d, t == i)))
     self_side = (side == d).astype(jnp.int32)
     expect = (
-        4 + 1 + up.astype(jnp.int32) + down.astype(jnp.int32) + 1
-        + (4 - self_side) + 4
+        4 + 1 + 5 * up.astype(jnp.int32) + 5 * down.astype(jnp.int32) + 1
+        + (4 - self_side) + 4 + (TP - self_side)
         + up.astype(jnp.int32) * (4 - self_side * (s == last // 2).astype(jnp.int32))
     )
 
+    loads[0].wait()
+    loads[1].wait()
+    blocks = width // BLOCK
+    eye = (
+        lax.broadcasted_iota(jnp.int32, (blocks, blocks), 0) == lax.broadcasted_iota(jnp.int32, (blocks, blocks), 1)
+    ).astype(F32).astype(BF16)
     for k in range(ticks):
-        for b in range(width // BLOCK):
+        scale = mm(stash_scales[k], eye, TN)
+        for b in range(blocks):
             cols = pl.ds(b * BLOCK, BLOCK)
-            scale = stash_scales[0, k, :, b : b + 1].astype(F32)
-            rest[k, :, cols] = (stash_values[0, k, :, cols].astype(F32) * scale).astype(BF16)
-    gain[...] = gains[:, pl.ds(pl.multiple_of(d * half, half), half)]
-
+            rest[k, :, cols] = (stash_values[k, :, cols].astype(F32) * scale[:, b : b + 1]).astype(BF16)
+
+    loads[2].wait()
+    loads[3].wait()
     pl.semaphore_wait(barrier, expect)
 
     piece_cols = pl.ds(pl.multiple_of(quarter * width, width), width)
@@ -171,25 +195,59 @@
                 dev(sec, 4 * d + i, side), cond, mine,
             )
 
-    to_slots(act_first.at[0], A.at[0], ("A", 0), s)
-    to_slots(grad_first.at[0], U.at[0], ("U", 0), s)
-    for k in range(ticks):
+    to_slots(act_first, A.at[0], ("A", 0), s)
+    to_slots(rest.at[0], R.at[0], ("R", 0), last - s, other=True)
+    to_slots(grad_first, U.at[0], ("U", 0), s)
+    loads[4].wait()
+    loads[5].wait()
+    loads[6].wait()
+
+    def later_slots(k):
         to_slots(rest.at[k], R.at[k], ("R", k), last - s, other=True)
-    push(act_first.at[0], raw.at[0], ("raw", 0), dev(last - s, t, d))
-    for k in range(1, ticks):
         to_slots(act_fresh.at[k - 1], A.at[k], ("A", k), s, s == 0)
         to_slots(grad_fresh.at[k - 1], U.at[k], ("U", k), s, s == last)
+        if k == 1:
+            push(act_first, raw.at[0], ("raw", 0), dev(last - s, t, d))
 
     def rows_of(j):
         return pl.ds(rows * j, rows)
 
-    def gather_start(X, key):
-        arrived(X.at[rows_of(0)], key)
-        own = X.at[rows_of(0)]
-        push(own, X.at[rows_of(2)], key + (2,), dev(s, ztp(-2), d))
-        push(own, X.at[rows_of(6)], key + (6,), dev(s, ztp(2), d))
-        push(own, X.at[rows_of(1)], key + (1,), dev(s, ztp(-1), d))
-        push(own, X.at[rows_of(7)], key + (7,), dev(s, ztp(1), d))
+    def spread(src, X, key, sec, cond=None, whole=True):
+        push(src, X.at[rows_of(2)], key + (2,), dev(sec, ztp(-2), d), cond)
+        push(src, X.at[rows_of(6)], key + (6,), dev(sec, ztp(2), d), cond)
+        push(src, X.at[rows_of(1)], key + (1,), dev(sec, ztp(-1), d), cond)
+        push(src, X.at[rows_of(7)], key + (7,), dev(sec, ztp(1), d), cond)
+        if whole:
+            push(src, X.at[rows_of(0)], key, dev(sec, t, d), cond)
+
+    def gather_start(X, key, cond=None):
+        def first():
+            arrived(X.at[rows_of(0)], key)
+
+        if cond is None:
+            first()
+        else:
+            pl.when(cond)(first)
+        spread(X.at[rows_of(0)], X, key, s, cond, False)
+
+    def chain(X, key, step):
+        if step == 0:
+            arrived(X.at[rows_of(0)], key)
+            push(X.at[rows_of(0)], X.at[rows_of(1)], key + (1,), dev(s, ztp(-1), d))
+            push(X.at[rows_of(0)], X.at[rows_of(7)], key + (7,), dev(s, ztp(1), d))
+        elif step < 3:
+            arrived(X.at[rows_of(step)], key + (step,))
+            push(X.at[rows_of(step)], X.at[rows_of(step + 1)], key + (step + 1,), dev(s, ztp(-1), d))
+            arrived(X.at[rows_of(8 - step)], key + (8 - step,))
+            push(X.at[rows_of(8 - step)], X.at[rows_of(7 - step)], key + (7 - step,), dev(s, ztp(1), d))
+        elif step == 3:
+            arrived(X.at[rows_of(3)], key + (3,))
+            push(X.at[rows_of(3), pl.ds(0, hw)], X.at[rows_of(4), pl.ds(0, hw)], key + (4,), dev(s, ztp(-1), d))
+            arrived(X.at[rows_of(5)], key + (5,))
+            push(X.at[rows_of(5), pl.ds(hw, hw)], X.at[rows_of(4), pl.ds(hw, hw)], key + (8,), dev(s, ztp(1), d))
+        else:
+            arrived(X.at[rows_of(4), pl.ds(0, hw)], key + (4,))
+            arrived(X.at[rows_of(4), pl.ds(hw, hw)], key + (8,))
 
     def gather_mid(X, key):
         arrived(X.at[rows_of(2)], key + (2,))
@@ -199,7 +257,9 @@
         push(X.at[rows_of(6)], X.at[rows_of(5)], key + (5,), dev(s, ztp(1), d))
         push(X.at[rows_of(6), pl.ds(hw, hw)], X.at[rows_of(4), pl.ds(hw, hw)], key + (8,), dev(s, ztp(2), d))
 
-    def gather_end(X, key):
+    def gather_end(X, key, cond=None):
+        if cond is not None:
+            pl.when(cond)(lambda: arrived(X.at[rows_of(0)], key))
         for j in (1, 7, 3, 5):
             arrived(X.at[rows_of(j)], key + (j,))
         arrived(X.at[rows_of(4), pl.ds(0, hw)], key + (4,))
@@ -273,48 +333,60 @@
         BN[pl.ds(k * tokens, tokens)] = (R[k].astype(F32) * inv * gain[...]).astype(BF16)
 
     def quantize(k):
-        blocks = raw[k].astype(F32)
+        values = raw[k].astype(F32)
         scales = []
         for b in range(width // BLOCK):
-            block = blocks[:, b * BLOCK : (b + 1) * BLOCK]
+            block = values[:, b * BLOCK : (b + 1) * BLOCK]
             top = jnp.max(jnp.abs(block), axis=-1, keepdims=True)
             scale = (top / QUANT_TOP + SCALE_EPS).astype(BF16)
             out_values[0, k, :, pl.ds(b * BLOCK, BLOCK)] = (block / scale.astype(F32)).astype(BF16)
             scales.append(scale.astype(F32))
-        out_scales[0, k] = jnp.concatenate(scales, axis=1).astype(BF16)
+        out_scales[0, k] = mm(eye, jnp.concatenate(scales, axis=1).astype(BF16), NT).astype(BF16)
 
     scale_out = 1.0 / math.sqrt(ticks * tokens)
 
-    for k in range(ticks):
-        gather_start(A.at[k], ("A", k))
-        gather_start(U.at[k], ("U", k))
-        if k == 0:
-            gather_start(R.at[k], ("R", k))
-            load_in.wait()
-            load_out.wait()
+    def forward_gather(k):
+        gather_start(A.at[k], ("A", k), None if k == 0 else s == 0)
+
+    def forward_pass_on(k):
         gather_mid(A.at[k], ("A", k))
-        gather_mid(U.at[k], ("U", k))
-        if k == 0:
-            gather_mid(R.at[k], ("R", k))
-        gather_end(A.at[k], ("A", k))
-        f_part = project(A.at[k], 3 * k, ("xf", k))
-        gather_end(U.at[k], ("U", k))
-        g_part = mm(U[k], w_out[...], NT)
-        xs[3 * k + 2] = g_part.astype(BF16)
-        swap_send(3 * k + 2, ("xg", k))
-        if k == 0:
-            gather_end(R.at[k], ("R", k))
-            r_part = restore_project(k)
-        if k + 1 < ticks:
-            gather_start(R.at[k + 1], ("R", k + 1))
-        f_pre, _ = projected(f_part, 3 * k, ("xf", k))
-        hidden = (f_pre * sigmoid(f_pre)).astype(BF16)
+
+    def forward_project(k):
+        gather_end(A.at[k], ("A", k), None if k == 0 else s > 0)
+        return project(A.at[k], 3 * k, ("xf", k))
+
+    def forward_branch(k, part):
+        pre, _ = projected(part, 3 * k, ("xf", k))
+        hidden = (pre * sigmoid(pre)).astype(BF16)
         Fp[k] = mm(hidden, w_out[...], NN).astype(BF16)
         sum_start(Fp.at[k], Fr.at[k], fwd_width, ("F", k))
-        if k == 0:
-            restore_finish(k, r_part)
+
+    def forward_sum(k):
+        sum_mid(Fp.at[k], Fr.at[k], Fs.at[k], fwd_width, ("F", k))
+
+    def forward_leave(k):
+        Fl[k] = (A[k, rows_of(0)].astype(F32) + sum_end(Fp.at[k], Fr.at[k], ("F", k))).astype(BF16)
+        if k + 1 < ticks:
+            spread(Fl.at[k], A.at[k + 1], ("A", k + 1), s + 1, up)
+        else:
+            to_blocks(Fl.at[k], fin_a, ("fin_a",), s)
+
+    def backward_gather(k):
+        gather_start(U.at[k], ("U", k), None if k == 0 else s == last)
+
+    def backward_pass_on(k):
+        gather_mid(U.at[k], ("U", k))
+
+    def backward_project(k):
+        gather_end(U.at[k], ("U", k), None if k == 0 else s < last)
+        part = mm(U[k], w_out[...], NT)
+        xs[3 * k + 2] = part.astype(BF16)
+        swap_send(3 * k + 2, ("xg", k))
+        return part
+
+    def backward_branch(k, part):
         arrived(xr.at[3 * k + 2], ("xg", k))
-        grad_pre = ((g_part + xr[3 * k + 2].astype(F32)) * b_sg[k]).astype(BF16)
+        grad_pre = ((part + xr[3 * k + 2].astype(F32)) * b_sg[k]).astype(BF16)
         GP[pl.ds(k * tokens, tokens)] = grad_pre
         center = jnp.sum(grad_pre.astype(F32) * b_pre[k], axis=-1, keepdims=True)
         center_hi = center.astype(BF16).astype(F32)
@@ -322,83 +394,139 @@
         Bp[k, :, pl.ds(half, BLOCK)] = jnp.where(lane < BLOCK // 2, center_hi, center - center_hi).astype(BF16)
         Bp[k, :, pl.ds(0, half)] = mm(grad_pre, w_in[...], NT).astype(BF16)
         sum_start(Bp.at[k], Br.at[k], bwd_width, ("B", k))
-        if k + 1 < ticks:
-            gather_mid(R.at[k + 1], ("R", k + 1))
-        sum_mid(Fp.at[k], Fr.at[k], Fs.at[k], fwd_width, ("F", k))
+
+    def backward_sum(k):
         sum_mid(Bp.at[k], Br.at[k], Bs.at[k], bwd_width, ("B", k))
-        if k + 1 < ticks:
-            gather_end(R.at[k + 1], ("R", k + 1))
-            r_part = restore_project(k + 1)
-        leaving = (A[k, rows_of(0)].astype(F32) + sum_end(Fp.at[k], Fr.at[k], ("F", k))).astype(BF16)
-        Fl[k] = leaving
-        if k + 1 < ticks:
-            push(Fl.at[k], A.at[k + 1, rows_of(0)], ("A", k + 1), dev(s + 1, t, d), up)
-            to_blocks(Fl.at[k], raw.at[k + 1], ("raw", k + 1), last - 1 - s, up, s == last // 2)
-        else:
-            to_blocks(Fl.at[k], fin_a, ("fin_a",), s)
+
+    def backward_leave(k):
         total = sum_end(Bp.at[k], Br.at[k], ("B", k))
         grad_normed = total[:, :half]
         center = total[:, half : half + 1] + total[:, half + BLOCK // 2 : half + BLOCK // 2 + 1]
         inv = unit_scale[k, rows_of(0)][:, 0:1]
         unit = R[k, rows_of(0)].astype(F32) * inv
         grads = grad_normed * gain[...] - unit * (center * (1.0 / model))
-        leaving = (U[k, rows_of(0)].astype(F32) + inv * grads).astype(BF16)
-        Bl[k] = leaving
+        Bl[k] = (U[k, rows_of(0)].astype(F32) + inv * grads).astype(BF16)
         if k + 1 < ticks:
-            push(Bl.at[k], U.at[k + 1, rows_of(0)], ("U", k + 1), dev(s - 1, t, d), down)
+            spread(Bl.at[k], U.at[k + 1], ("U", k + 1), s - 1, down)
         else:
             to_blocks(Bl.at[k], fin_g, ("fin_g",), s)
         terms = grad_normed * unit
         terms = terms[0:8] + terms[8:16]
         gacc[...] = terms if k == 0 else gacc[...] + terms
-        if k + 1 < ticks:
-            restore_finish(k + 1, r_part)
-
+
+    def grad_out_weights():
+        step = 256
+        for i in range(inner // step):
+            cols = pl.ds(i * step, step)
+            total = mm(BH[pl.ds(0, tokens), cols], U[0], TN)
+            for k in range(1, ticks):
+                total = total + mm(BH[pl.ds(k * tokens, tokens), cols], U[k], TN)
+            grad_out_w[0, cols, :] = (total * scale_out).astype(BF16)
+
+    def grad_in_weights():
+        step = 256
+        for i in range(half // step):
+            cols = pl.ds(i * step, step)
+            grad_in_w[0, cols, :] = (mm(BN[:, cols], GP[...], TN) * scale_out).astype(BF16)
+
+    def stash_out(k):
+        if k == 0:
+            arrived(raw.at[0], ("raw", 0))
+        else:
+
+            @pl.when(s < last)
+            def _():
+                arrived(raw.at[k], ("raw", k))
+
+            @pl.when(s == last)
+            def _():
+                raw[k] = act_fresh[k - 1]
+
+        quantize(k)
+
+    for k in range(ticks):
+        more = k + 1 < ticks
+        forward_gather(k)
+        if k == 0:
+            loads[7].wait()
+            loads[8].wait()
+        else:
+            backward_sum(k - 1)
+        forward_pass_on(k)
+        if k == 0:
+            backward_gather(0)
+            gather_start(R.at[0], ("R", 0))
+            later_slots(1)
+        else:
+            backward_leave(k - 1)
+            backward_gather(k)
+            to_blocks(Fl.at[k - 1], raw.at[k], ("raw", k), last - 1 - s, up, s == last // 2)
+            restore_finish(k, r_part)
+        f_part = forward_project(k)
+        if k > 0 and more:
+            gather_start(R.at[k + 1], ("R", k + 1))
+        if k == 0:
+            gather_mid(R.at[0], ("R", 0))
+        backward_pass_on(k)
+        if not more:
+            stash_out(0)
+        forward_branch(k, f_part)
+        if k == 0:
+            gather_end(R.at[0], ("R", 0))
+            r_part = restore_project(0)
+            gather_start(R.at[1], ("R", 1))
+        if k + 2 < ticks:
+            later_slots(k + 2)
+        g_part = backward_project(k)
+        if not more:
+            stash_out(1)
+        if more:
+            gather_mid(R.at[k + 1], ("R", k + 1))
+        forward_sum(k)
+        if k == 0:
+            restore_finish(0, r_part)
+        if not more:
+            stash_out(2)
+        backward_branch(k, g_part)
+        if more:
+            gather_end(R.at[k + 1], ("R", k + 1))
+            r_part = restore_project(k + 1)
+        else:
+            grad_out_weights()
+        forward_leave(k)
+    backward_sum(ticks - 1)
+    grad_in_weights()
+    backward_leave(ticks - 1)
     for i in range(4):
-        push(
-            gacc.at[:, pl.ds(i * width, width)], gpieces.at[quarter], ("gp",), dev(s, 4 * d + i, side), None, is_own(i)
-        )
-    step = 256
-    for i in range(half // step):
-        cols = pl.ds(i * step, step)
-        grad_in_w[0, cols, :] = (mm(BN[:, cols], GP[...], TN) * scale_out).astype(BF16)
-    arrived(gpieces, ("gp",))
-    group = jnp.sum(gpieces[0] + gpieces[1] + gpieces[2] + gpieces[3], axis=0, keepdims=True)
-    gsum[...] = jnp.broadcast_to(group.astype(BF16).astype(F32), gsum.shape)
-    part_width = width // DP
-    mine = pl.ds(pl.multiple_of(d * part_width, part_width), part_width)
-    theirs = pl.ds(pl.multiple_of((1 - d) * part_width, part_width), part_width)
-    push(gsum.at[:, theirs], grecv, ("gx",), dev(s, t, 1 - d))
-    for i in range(inner // step):
-        cols = pl.ds(i * step, step)
-        total = mm(BH[pl.ds(0, tokens), cols], U[0], TN)
-        for k in range(1, ticks):
-            total = total + mm(BH[pl.ds(k * tokens, tokens), cols], U[k], TN)
-        grad_out_w[0, cols, :] = (total * scale_out).astype(BF16)
-    arrived(raw.at[0], ("raw", 0))
-    for k in range(1, ticks):
-
-        @pl.when(s < last)
-        def _():
-            arrived(raw.at[k], ("raw", k))
-
-        @pl.when(s == last)
-        def _():
-            raw[k] = act_fresh[k - 1]
-
-    for k in range(ticks):
-        quantize(k)
+        for e in range(DP):
+            push(
+                gacc.at[:, pl.ds(i * width + e * (width // DP), width // DP)], gpieces.at[t], ("gp",),
+                dev(s, 4 * d + i, e), None, jnp.logical_and(is_own(i), d == e),
+            )
     arrived(fin_a, ("fin_a",))
     act_out[0] = fin_a[...]
     arrived(fin_g, ("fin_g",))
     grad_out[0] = fin_g[...]
-    arrived(grecv, ("gx",))
-    grad_gain[...] = ((gsum[:, mine] + grecv[...]) * scale_out)[0:1]
+    arrived(gpieces, ("gp",))
+    groups = [
+        jnp.sum(sum(gpieces[4 * g + i] for i in range(4)), axis=0, keepdims=True).astype(BF16).astype(F32)
+        for g in range(DP)
+    ]
+    grad_gain[...] = (groups[0] + groups[1]) * scale_out
     for copy, cond in pending:
         if cond is None:
             copy.wait_send()
         else:
             pl.when(cond)(copy.wait_send)
+
+
+def store_kernel(*refs):
+    count = len(refs) // 2
+    copies = [pltpu.make_async_copy(refs[i], refs[count + i], refs[-1].at[i]) for i in range(count)]
+    for copy in copies:
+        copy.start()
+    for copy in copies:
+        copy.wait()
 
 
 def local(act_first, act_fresh, grad_first, grad_fresh, stash_values, stash_scales, gains, w_in, w_out):
@@ -408,27 +536,34 @@
     half, inner = w_in.shape[1:]
     tokens = tok * DP
     rows = tokens // TP
+    scales = jnp.swapaxes(stash_scales, 2, 3)
     vmem = pl.BlockSpec(memory_space=pltpu.VMEM)
     hbm = pl.BlockSpec(memory_space=pl.ANY)
     bw = half + BLOCK
     V = pltpu.VMEM
-    return pl.pallas_call(
+    outs = pl.pallas_call(
         functools.partial(kernel, sections, ticks, tok, width, half, inner),
         out_shape=(
-            jax.ShapeDtypeStruct(act_first.shape, BF16),
-            jax.ShapeDtypeStruct(grad_first.shape, BF16),
-            jax.ShapeDtypeStruct(stash_values.shape, BF16),
-            jax.ShapeDtypeStruct(stash_scales.shape, BF16),
-            jax.ShapeDtypeStruct(w_in.shape, BF16),
-            jax.ShapeDtypeStruct(w_out.shape, BF16),
-            jax.ShapeDtypeStruct((1, width // DP), F32),
+            V(act_first.shape, BF16),
+            V(grad_first.shape, BF16),
+            V(stash_values.shape, BF16),
+            V(scales.shape, BF16),
+            V(w_in.shape, BF16),
+            V(w_out.shape, BF16),
+            V((1, width // DP), F32),
         ),
-        in_specs=[vmem] * 7 + [hbm] * 2,
+        in_specs=[hbm] * 9,
         out_specs=(vmem,) * 7,
         scratch_shapes=[
+            V((tok, width), BF16),
+            V(act_fresh.shape, BF16),
+            V((tok, width), BF16),
+            V(act_fresh.shape, BF16),
+            V((ticks, tok, width), BF16),
+            V(scales.shape[1:], BF16),
+            V((1, half), F32),
             V((half, inner), BF16),
             V((inner, half), BF16),
-            V((1, half), F32),
             V((ticks, tokens, half), BF16),
             V((ticks, tokens, half), BF16),
             V((ticks, tokens, half), BF16),
@@ -453,20 +588,31 @@
             V((ticks * tokens, inner), BF16),
             V((ticks, tokens, BLOCK), F32),
             V((8, half), F32),
-            V((4, 8, width), F32),
-            V((8, width), F32),
-            V((8, width // DP), F32),
+            V((TP, 8, width // DP), F32),
             V((tok, width), BF16),
             V((tok, width), BF16),
-            pltpu.SemaphoreType.DMA((2,)),
-            pltpu.SemaphoreType.DMA((224,)),
+            pltpu.SemaphoreType.DMA((9,)),
+            pltpu.SemaphoreType.DMA((232,)),
             pltpu.SemaphoreType.DMA((160,)),
         ],
         compiler_params=pltpu.CompilerParams(
-            collective_id=1, has_side_effects=True, vmem_limit_bytes=56 * 2**20
+            collective_id=1, has_side_effects=True, vmem_limit_bytes=59 * 2**20
         ),
         name="relay_window",
-    )(act_first, act_fresh, grad_first, grad_fresh, stash_values, stash_scales, gains, w_in, w_out)
+    )(act_first, act_fresh, grad_first, grad_fresh, stash_values, scales, gains, w_in, w_out)
+    outs = list(
+        pl.pallas_call(
+            store_kernel,
+            out_shape=tuple(jax.ShapeDtypeStruct(o.shape, o.dtype) for o in outs),
+            in_specs=[vmem] * len(outs),
+            out_specs=(hbm,) * len(outs),
+            scratch_shapes=[pltpu.SemaphoreType.DMA((len(outs),))],
+            compiler_params=pltpu.CompilerParams(vmem_limit_bytes=8 * 2**20),
+            name="store",
+        )(*outs)
+    )
+    outs[3] = jnp.swapaxes(outs[3], 2, 3)
+    return tuple(outs)
 
 
 def solution(mesh):

time: 186 us -> 163 us (0.88)
  local copies, waits for them, and re-layouts: 12.5 us -> 0 us
  Pallas kernels: 172 us -> 162 us
    pallas_call x1, Pallas kernels: 172 us -> 160 us  [local(): pl.pallas_call(functools.partial(kernel, sections, ticks, tok, width, hal...]
    unnamed x11 -> x0, local copies, waits for them, and re-layouts: 11.1 us -> none
    pallas_call x0 -> x1, Pallas kernels: none -> 2.19 us  [local(): pl.pallas_call(store_kernel, out_shape=tuple((jax.ShapeDtypeStruct(o.shap...]
where the time goes in v2:
time: 163 us
  Pallas kernels  162 us (99%)
    pallas_call x1, Pallas kernels, local(): pl.pallas_call(functools.partial(kernel, sections, ticks, tok, width, hal...  160 us

profile of v2, /device:TPU:2, one launch (start us, length us, event | category | flops | bytes accessed | tf_op | source)
XLA Modules:
  0.0 162.5 jit_solution(12224198037395333365)
XLA Ops:
  0.6 159.5 %relay_window.1 = (bf16[1,64,512]{2,1,0:T(8,128)(2,1)S(1)}, bf16[1,64,512]{2,1,0:T(8,128)(2,1)S(1)}, bf16[1,3,64,512]{3,2,1,0:T(8,128)(2,1)S(1)}, bf16[1,3,4,64]...) custom-call(bf16[1,64,512]{2,1,0:T(8,128)(2,1)} %act_first_h.1, ...), custom_call_target="tpu_custom_call" | custom-call | tf_op jit(solution)/shard_map/relay_window/pallas_call | solution.py:544
  160.2 2.2 %store.1 = (bf16[1,64,512]{2,1,0:T(8,128)(2,1)}, bf16[1,64,512]{2,1,0:T(8,128)(2,1)}, bf16[1,3,64,512]{3,2,1,0:T(8,128)(2,1)}, bf16[1,3,4,64]{3,2,1,0:T(4,128)(2...) custom-call(bf16[1,64,512]{2,1,0:T(8,128)(2,1)S(1)} %get-tuple-element.21.refs_0_, ...), custom_call_target="tpu_custom_call" | custom-call | tf_op jit(solution)/shard_map/store/pallas_call | solution.py:604

commit v3 on v2

--- a/solution.py
+++ b/solution.py
@@ -452,6 +452,7 @@
             loads[8].wait()
         else:
             backward_sum(k - 1)
+            chain(R.at[k], ("R", k), 2)
         forward_pass_on(k)
         if k == 0:
             backward_gather(0)
@@ -461,27 +462,27 @@
             backward_leave(k - 1)
             backward_gather(k)
             to_blocks(Fl.at[k - 1], raw.at[k], ("raw", k), last - 1 - s, up, s == last // 2)
-            restore_finish(k, r_part)
+            chain(R.at[k], ("R", k), 3)
         f_part = forward_project(k)
-        if k > 0 and more:
-            gather_start(R.at[k + 1], ("R", k + 1))
+        if k > 0:
+            chain(R.at[k], ("R", k), 4)
+            r_part = restore_project(k)
         if k == 0:
             gather_mid(R.at[0], ("R", 0))
         backward_pass_on(k)
         if not more:
             stash_out(0)
         forward_branch(k, f_part)
+        if k > 0:
+            restore_finish(k, r_part)
         if k == 0:
             gather_end(R.at[0], ("R", 0))
             r_part = restore_project(0)
-            gather_start(R.at[1], ("R", 1))
         if k + 2 < ticks:
             later_slots(k + 2)
         g_part = backward_project(k)
         if not more:
             stash_out(1)
-        if more:
-            gather_mid(R.at[k + 1], ("R", k + 1))
         forward_sum(k)
         if k == 0:
             restore_finish(0, r_part)
@@ -489,11 +490,12 @@
             stash_out(2)
         backward_branch(k, g_part)
         if more:
-            gather_end(R.at[k + 1], ("R", k + 1))
-            r_part = restore_project(k + 1)
+            chain(R.at[k + 1], ("R", k + 1), 0)
         else:
             grad_out_weights()
         forward_leave(k)
+        if more:
+            chain(R.at[k + 1], ("R", k + 1), 1)
     backward_sum(ticks - 1)
     grad_in_weights()
     backward_leave(ticks - 1)

time: 163 us -> 162 us (level)
  no operation moved by 1% of the time
where the time goes in v3:
time: 162 us; the launch traced here: 161 us
  Pallas kernels  161 us (99%)
    pallas_call x1, Pallas kernels, local(): pl.pallas_call(functools.partial(kernel, sections, ticks, tok, width, hal...  158 us

profile of v3, /device:TPU:2, one launch (start us, length us, event | category | flops | bytes accessed | tf_op | source)
XLA Modules:
  0.0 161.5 jit_solution(5381929326265604043)
XLA Ops:
  0.6 158.5 %relay_window.1 = (bf16[1,64,512]{2,1,0:T(8,128)(2,1)S(1)}, bf16[1,64,512]{2,1,0:T(8,128)(2,1)S(1)}, bf16[1,3,64,512]{3,2,1,0:T(8,128)(2,1)S(1)}, bf16[1,3,4,64]...) custom-call(bf16[1,64,512]{2,1,0:T(8,128)(2,1)} %act_first_h.1, ...), custom_call_target="tpu_custom_call" | custom-call | tf_op jit(solution)/shard_map/relay_window/pallas_call | solution.py:546
  159.1 2.2 %store.1 = (bf16[1,64,512]{2,1,0:T(8,128)(2,1)}, bf16[1,64,512]{2,1,0:T(8,128)(2,1)}, bf16[1,3,64,512]{3,2,1,0:T(8,128)(2,1)}, bf16[1,3,4,64]{3,2,1,0:T(4,128)(2...) custom-call(bf16[1,64,512]{2,1,0:T(8,128)(2,1)S(1)} %get-tuple-element.21.refs_0_, ...), custom_call_target="tpu_custom_call" | custom-call | tf_op jit(solution)/shard_map/store/pallas_call | solution.py:606
